TPU v7x, 128 devices: a whole 4x4x4 slice. The times are simulated.
128 devices in a mesh: dp: 8 (over z, x_lo), owner: 16 (over x_hi, y, core).
Axes of the slice: x: 4 (x_hi: 2, x_lo: 2; x = x_hi * 2 + x_lo), y: 4, z: 4, core: 2. Of those that a mesh axis runs over, the one named last changes fastest.
Arguments:
- activations: bfloat16 [131072, 8192], P(('dp', 'owner')), may hold values from -12 to 12
- gradient: bfloat16 [8192, 4096], P(None, ('dp', 'owner')), may hold values from -6 to 6
- iterations: int32 [32], replicated, may hold values from 5 to 8
Outputs:
- preconditioned: bfloat16 [8192, 4096], P(None, 'dp')
All inputs are finite; a program needn't handle non-finite values. Where the computation divides by a largest or mean magnitude, that divisor is 1e-20 or more.
Results may differ from a plain program's by a relative error of at most 0.012.
Values may be sent and summed in bfloat16 or wider, within the bound.
A program may use at most 192 MiB of HBM per device.

v0:
```python
import jax
import jax.numpy as jnp
from jax import lax
from jax.sharding import PartitionSpec as P

BS = 256


damping = 0.1


def newton_inverse(damped, count):
    identity = jnp.eye(damped.shape[0], dtype=jnp.float32)
    row_bound = jnp.max(jnp.sum(jnp.abs(damped), axis=1))

    def newton(step_index, approx):
        product = jnp.dot(damped, approx, precision=lax.Precision.HIGHEST)
        return 2.0 * approx - jnp.dot(approx, product, precision=lax.Precision.HIGHEST)

    return lax.fori_loop(0, count, newton, identity / row_bound)


def per_device(activations, gradient, iterations):
    owners = lax.axis_size("owner")
    shards = lax.axis_size("dp")
    rows_here, width = activations.shape
    blocks = width // BS
    per_owner = blocks // owners
    rows_total = rows_here * owners * shards
    block_order = jnp.arange(blocks, dtype=jnp.int32)
    features = activations.reshape(rows_here, blocks, BS)
    partial_value = jnp.einsum(
        "tnb,tnc->nbc", features, features, preferred_element_type=jnp.float32
    )
    factor = lax.psum_scatter(
        partial_value.astype(jnp.bfloat16), "owner", scatter_dimension=0, tiled=True
    ).astype(jnp.float32)
    factor = lax.psum(factor, "dp")
    identity = jnp.eye(BS, dtype=jnp.float32)
    owner_index = lax.axis_index("owner")
    held_ids = lax.dynamic_slice_in_dim(block_order, owner_index * per_owner, per_owner)
    held_counts = jnp.take(iterations, held_ids)
    inverses = []
    for slot_index in range(per_owner):
        damped = factor[slot_index] / rows_total + damping * identity
        inverses.append(newton_inverse(damped, held_counts[slot_index]))
    inverse = jnp.stack(inverses).astype(jnp.bfloat16)
    grad_cols = gradient.shape[1]
    grad_blocks = gradient.reshape(blocks, BS, grad_cols)
    held_rows = lax.all_to_all(grad_blocks, "owner", split_axis=0, concat_axis=2, tiled=True)
    panel = jnp.einsum(
        "kab,kbf->kaf", inverse, held_rows, preferred_element_type=jnp.float32
    ).astype(jnp.bfloat16)
    whole = lax.all_gather(panel, "owner", axis=0, tiled=True)
    return whole.reshape(blocks * BS, whole.shape[2])


def solution(mesh):
    placed = (P(("dp", "owner"), None), P(None, ("dp", "owner")), P())
    return jax.shard_map(
        per_device, mesh=mesh, in_specs=placed, out_specs=P(None, "dp"), check_vma=False
    )
```

profile of v0, /device:TPU:1, one launch (start us, length us, event | category | flops | bytes accessed | tf_op | source)
XLA Modules:
  0.0 264.9 jit_solution(13878470498093350481)
XLA Ops:
  6.5 14.7 %fusion.5 = bf16[32,256,256]{2,1,0:T(8,128)(2,1)} fusion(bf16[128,32,8,256]{3,2,1,0:T(8,128)(2,1)} %bitcast.78), kind=kOutput, calls=%fused_computation.8 | convolution fusion | flops 4297064448 | bytes 20971520 | tf_op jit(solution)/shard_map/tnb,tnc->nbc/dot_general | solution.py:32
  21.2 0.9 copy.46
  22.1 8.4 %all-to-all-start = ((bf16[32,256,32]{1,2,0:T(8,128)(2,1)}), bf16[32,256,32]{1,2,0:T(8,128)(2,1)S(1)}, u32[]{:S(2)}, u32[]{:S(2)}) async-start(bf16[32,256,32]{1,2,0:T(8,128)(2,1)} %bitcast.51), calls=%async_computation.1 | async-start | bytes 1048576 | tf_op jit(solution)/shard_map/all_to_all | solution.py:50
  30.7 0.6 gather_fusion
  31.4 0.7 fusion.16
  32.1 9.8 %all-to-all-done = bf16[32,256,32]{1,2,0:T(8,128)(2,1)S(1)} async-done(((bf16[32,256,32]{1,2,0:T(8,128)(2,1)}), bf16[32,256,32]{1,2,0:T(8,128)(2,1)S(1)}, u32[]{:S(2)}, u32[]{:S(2)}) %all-to-all-start) | async-done | bytes 524320 | tf_op jit(solution)/shard_map/all_to_all | solution.py:50
  41.9 61.9 %reduce-scatter.2.cloned.1.call-done = bf16[2,256,256]{2,1,0:T(8,128)(2,1)} async-done(((bf16[32,256,256]{2,1,0:T(8,128)(2,1)}), bf16[2,256,256]{2,1,0:T(8,128)(2,1)}) %reduce-scatter.2.cloned.1.call-update) | async-done | bytes 262160 | tf_op jit(solution)/shard_map/reduce_scatter | solution.py:35
  103.7 38.7 %all-reduce.1 = f32[2,256,256]{2,1,0:T(8,128)S(1)} all-reduce(bf16[2,256,256]{2,1,0:T(8,128)(2,1)} %reduce-scatter.2.cloned.1.call-done), channel_id=1, replica_groups=mesh['dp'=8,'owner'=16] {'dp'}, use_global_device_ids=true, to_apply=%region_1.0 | all-reduce | flops 131072 | bytes 786432 | tf_op jit(solution)/shard_map/psum | solution.py:38
  142.6 0.6 reduce_max.19
  143.2 0.7 reduce_max.18
  145.4 9.1 %while.20 = (s32[]{:T(128)}, f32[256,256]{0,1:T(8,128)S(1)}, s32[]{:T(128)}, f32[256,256]{1,0:T(8,128)S(1)}, s32[]{:T(128)}) while((s32[]{:T(128)}, f32[256,256]{0,1:T(8,128)S(1)}, s32[]{:T(128)}, f32[256,256]{1,0:T(8,128)S(1)}, s32[]{:T(128)}) %tuple.46), condition=%wide.region_5.6_spmd, body=%wide.region_4.5_spmd.sunk | while | flops 402784256 | bytes 2097213 | solution.py:20
  146.1 0.4 fusion.44
  146.5 0.6 fusion.45
  148.2 0.6 fusion.45
  149.9 0.6 fusion.45
  151.6 0.6 fusion.45
  152.9 0.4 fusion.44
  153.3 0.6 fusion.45
  154.9 14.2 %while.21 = (s32[]{:T(128)}, f32[256,256]{0,1:T(8,128)S(1)}, s32[]{:T(128)}, f32[256,256]{1,0:T(8,128)S(1)}, s32[]{:T(128)}) while((s32[]{:T(128)}, f32[256,256]{0,1:T(8,128)S(1)}, s32[]{:T(128)}, f32[256,256]{1,0:T(8,128)S(1)}, s32[]{:T(128)}) %tuple.43), condition=%wide.region_9.10_spmd, body=%wide.region_8.9_spmd.sunk | while | flops 402784256 | bytes 2097213 | solution.py:20
  155.9 0.6 fusion.51
  157.6 0.6 fusion.51
  158.9 0.4 fusion.50
  159.3 0.6 fusion.51
  160.6 0.4 fusion.50
  161.0 0.6 fusion.51
  162.7 0.6 fusion.51
  164.4 0.6 fusion.51
  166.1 0.6 fusion.51
  167.8 0.6 fusion.51
  169.1 1.1 convolution_convert_fusion
  170.3 80.5 %all-gather.2.cloned.1.call-done = bf16[32,256,512]{2,1,0:T(8,128)(2,1)} async-done(((bf16[2,256,512]{2,1,0:T(8,128)(2,1)}), bf16[32,256,512]{2,1,0:T(8,128)(2,1)}) %all-gather.2.cloned.1.call-update) | async-done | bytes 8388624 | tf_op jit(solution)/shard_map/all_gather | solution.py:54
  250.8 7.3 %copy.67 = bf16[8192,512]{1,0:T(8,128)(2,1)} copy(bf16[8192,512]{1,0:T(8,128)(2,1)} %bitcast.72) | data formatting | bytes 16777216
  (42 shorter events, 4.9 us)
Async XLA Ops:
  6.5 24.2 %copy-start = (s32[32]{0:T(128)S(1)}, s32[32]{0:T(128)}, u32[]{:S(2)}) copy-start(s32[32]{0:T(128)} %param.9) | copy-start | bytes 388
  6.5 97.2 %reduce-scatter.2.cloned.1.call-start = ((), (), s32[]{:S(2)}) async-start(), calls=%async_computation.2 | async-start | bytes 4456448 | tf_op jit(solution)/shard_map/reduce_scatter | solution.py:35
  6.5 14.7 %copy-start.1 = (bf16[8192,32]{0,1:T(8,128)(2,1)S(1)}, bf16[8192,32]{0,1:T(8,128)(2,1)}, u32[]{:S(2)}) copy-start(bf16[8192,32]{0,1:T(8,128)(2,1)} %param.8) | copy-start | bytes 1572868
  22.1 19.7 %all-to-all-start = ((bf16[32,256,32]{1,2,0:T(8,128)(2,1)}), bf16[32,256,32]{1,2,0:T(8,128)(2,1)S(1)}, u32[]{:S(2)}, u32[]{:S(2)}) async-start(bf16[32,256,32]{1,2,0:T(8,128)(2,1)} %bitcast.51), calls=%async_computation.1 | async-start | bytes 1048576 | tf_op jit(solution)/shard_map/all_to_all | solution.py:50
  30.5 220.2 %all-gather.2.cloned.1.call-start = ((), (), s32[]{:S(2)}) async-start(), calls=%async_computation.3 | async-start | bytes 8912896 | tf_op jit(solution)/shard_map/all_gather | solution.py:54
Sparse Core Ops, SparseCore 0:
  21.4 82.3 reduce-scatter.1
  170.4 80.2 all-gather.1
where the time goes:
time: 265 us
  waiting for transfers between devices  152 us (57%)
  blocking collectives  38.7 us (15%)
  matrix products  28.9 us (11%)
  between operations  14.9 us (6%)
  local copies, waits for them, and re-layouts  10.2 us (4%)
  loops' own time  9.98 us (4%)
  starting transfers between devices  8.49 us (3%)
    all_gather x1, waiting for transfers between devices, per_device(): whole = lax.all_gather(panel, 'owner', axis=0, tiled=True)  80.5 us
    reduce_scatter x1, waiting for transfers between devices, per_device(): lax.psum_scatter(partial_value.astype(jnp.bfloat16), 'owner', scatter_dim...  61.9 us
    psum x1, blocking collectives, per_device(): factor = lax.psum(factor, 'dp')  38.7 us
    dot_general x1, matrix products, per_device(): jnp.einsum('tnb,tnc->nbc', features, features, preferred_element_type=jnp...  14.7 us
    another operation x2, loops' own time, newton_inverse(): return lax.fori_loop(0, count, newton, identity / row_bound)  9.98 us
    all_to_all x1, waiting for transfers between devices, per_device(): lax.all_to_all(grad_blocks, 'owner', split_axis=0, concat_axis=2, tiled=T...  9.78 us
    all_to_all x1, starting transfers between devices, per_device(): lax.all_to_all(grad_blocks, 'owner', split_axis=0, concat_axis=2, tiled=T...  8.45 us
    dot_general x13, matrix products, newton(): jnp.dot(approx, product, precision=lax.Precision.HIGHEST)  7.75 us
  transfers between devices with their start and end apart: 3, of which 3 were waited for; matrix products, arithmetic and copies ran while one was open for 1% of the time, Pallas kernels for 0%

commit v1 on v0

v1 whole, which is shorter than its diff:
```python
import functools

import jax
import jax.numpy as jnp
from jax import lax
from jax.experimental import pallas as pl
from jax.experimental.pallas import tpu as pltpu
from jax.sharding import PartitionSpec as P

BS = 256
HALF = BS // 2
BLOCKS = 32
PACK = BS + 16
TOKENS = 131072
DAMPING = 0.1
ITERS = 8
LEAST_ITERS = 5
SIDE = 4
GROUP = 4
GROUP_COLS = GROUP * BS
CLASS = 16
MESH = pl.DeviceIdType.MESH

TN = (((0,), (0,)), ((), ()))
NT = (((1,), (1,)), ((), ()))


def here():
    shard = lax.axis_index("dp")
    owner = lax.axis_index("owner")
    x = (owner // 8) * 2 + shard % 2
    return x, (owner // 2) % 4, shard // 2, owner % 2


def mesh_id(x, y, z, core):
    return (z * 2 + x % 2, (x // 2) * 8 + y * 2 + core)


def owner_of(x, y, core):
    return (x // 2) * 8 + y * 2 + core


def tile_iota():
    rows = lax.broadcasted_iota(jnp.int32, (HALF, HALF), 0)
    cols = lax.broadcasted_iota(jnp.int32, (HALF, HALF), 1)
    return rows, cols


def pack(block):
    rows, cols = tile_iota()
    low = block[HALF:, HALF:]
    mixed = jnp.where(rows <= cols, block[:HALF, :HALF], low)
    diagonal = jnp.sum(jnp.where(rows == cols, low, 0.0), axis=0, keepdims=True)
    return mixed, block[:HALF, HALF:], jnp.broadcast_to(diagonal, (16, HALF))


def unpack(mixed, off, diagonal):
    rows, cols = tile_iota()
    turned = mixed.T
    first = jnp.where(rows <= cols, mixed, turned)
    second = jnp.where(rows > cols, mixed, jnp.where(rows < cols, turned, diagonal))
    return first, off, off.T, second


def split(value):
    high = value.astype(jnp.bfloat16)
    return high, (value - high.astype(jnp.float32)).astype(jnp.bfloat16)


def dot3(left, right):
    lh, ll = split(left)
    rh, rl = split(right)
    mul = functools.partial(jnp.dot, preferred_element_type=jnp.float32)
    return mul(lh, rh) + (mul(lh, rl) + mul(ll, rh))


def newton(factor, count):
    rows = lax.broadcasted_iota(jnp.int32, (BS, BS), 0)
    cols = lax.broadcasted_iota(jnp.int32, (BS, BS), 1)
    identity = jnp.where(rows == cols, 1.0, 0.0)
    damped = factor / TOKENS + DAMPING * identity
    bound = jnp.max(jnp.sum(jnp.abs(damped), axis=1))
    ratio = damped / bound
    approx = (2.0 * identity - ratio) / bound
    ratio = 2.0 * ratio - dot3(ratio, ratio)
    for step in range(1, ITERS):
        if step < ITERS - 1:
            both = dot3(jnp.concatenate([ratio, approx], axis=0), ratio)
            later = 2.0 * approx - both[BS:]
            ratio = 2.0 * ratio - both[:BS]
        else:
            later = 2.0 * approx - dot3(approx, ratio)
        approx = later if step < LEAST_ITERS else jnp.where(step < count, later, approx)
    return approx


def factor_kernel(
    act_ref, grad_ref, iters_ref,
    full_ref, inv_ref,
    act, to_sib, from_sib, own, summed, landed, y_terms, inv_own,
    act_sem, sib_send, sib_recv, rs_send, rs_recv, y_send, y_recv,
    ag_send, ag_recv, ags_send, ags_recv,
    g_local, g_send, g_recv, gs_send, gs_recv,
):
    x, y, z, core = here()
    sibling = mesh_id(x, y, z, 1 - core)

    def at(dx, dy, dz):
        return mesh_id((x + dx) % SIDE, (y + dy) % SIDE, (z + dz) % SIDE, core)

    plane = [(dz, dx) for dz in (1, 2, 3, 0) for dx in range(SIDE) if dz or dx]

    def remote(src, dst, send, recv, target):
        return pltpu.make_async_remote_copy(
            src_ref=src, dst_ref=dst, send_sem=send, recv_sem=recv, device_id=target, device_id_type=MESH
        )

    def act_copy(slot):
        side = jnp.where(slot < 4, 1 - core, core)
        group = side * 4 + (z + slot % 4 + 1) % SIDE
        cols = pl.ds(pl.multiple_of(group * GROUP_COLS, GROUP_COLS), GROUP_COLS)
        return pltpu.make_async_copy(act_ref.at[:, cols], act.at[slot], act_sem.at[slot])

    for slot in range(8):
        act_copy(slot).start()

    barrier = pltpu.get_barrier_semaphore()
    partners = [sibling] + [at(dx, 0, dz) for dz, dx in plane] + [at(0, dy, 0) for dy in (1, 2, 3)]
    for partner in partners:
        pl.semaphore_signal(barrier, inc=1, device_id=partner, device_id_type=MESH)
    pl.semaphore_wait(barrier, len(partners))

    def rows_of(dx, dy, side):
        first = owner_of((x + dx) % SIDE, (y + dy) % SIDE, side) * 32
        return pl.ds(pl.multiple_of(first, 32), 32)

    def shard(dx, dy, side=core):
        return full_ref.at[rows_of(dx, dy, side)]

    mine = pltpu.make_async_copy(grad_ref, shard(0, 0), g_local)
    mine.start()
    g_copies = []
    first_copy = remote(grad_ref, shard(0, 0), g_send.at[0], g_recv.at[0], at(2, 0, 0))
    first_copy.start()
    for dy in (1, 3, 2):
        copy = remote(grad_ref, shard(0, 0), g_send.at[dy], g_recv.at[dy], at(0, dy, 0))
        copy.start()
        g_copies.append(copy)
    own_to_sib = remote(grad_ref, shard(0, 0), gs_send.at[0], gs_recv.at[0], sibling)
    own_to_sib.start()

    def products(slot, store):
        act_copy(slot).wait()
        for j in range(GROUP):
            cols = act[slot, :, j * BS : (j + 1) * BS]
            mixed, off, diagonal = pack(lax.dot_general(cols, cols, TN, preferred_element_type=jnp.float32))
            store(j, 0, HALF, mixed)
            store(j, HALF, HALF, off)
            store(j, BS, 16, diagonal)

    def sib_copy(k):
        return remote(to_sib.at[k], from_sib.at[k], sib_send.at[k], sib_recv.at[k], sibling)

    def sibling_group(k, carry):
        def store(j, first, rows, value):
            to_sib[k, j, pl.ds(first, rows), :] = value.astype(jnp.bfloat16)

        products(k, store)
        sib_copy(k).start()
        return carry

    lax.fori_loop(0, 4, sibling_group, 0)

    def rs_copy(dz, dx):
        k = (dz + 3) % 4
        slot = dz * 4 + dx
        return remote(
            summed.at[k, (x + dx) % SIDE], landed.at[slot], rs_send.at[slot], rs_recv.at[slot], at(dx, 0, dz)
        )

    def own_products(k):
        def store(j, first, rows, value):
            own[j, pl.ds(first, rows), :] = value

        products(4 + k, store)
        sib_copy(k).wait_recv()
        summed[k] = (own[...] + from_sib[k].astype(jnp.float32)).astype(jnp.bfloat16)

    for k in range(4):
        own_products(k)
        for dx in range(SIDE):
            if k < 3 or dx:
                rs_copy((k + 1) % 4, dx).start()

    first_copy.wait_recv()
    second_copies = []
    for dy in (1, 3, 2):
        copy = remote(shard(2, 0), shard(2, 0), g_send.at[3 + dy], g_recv.at[3 + dy], at(0, dy, 0))
        copy.start()
        second_copies.append(copy)
    partner_to_sib = remote(shard(2, 0), shard(2, 0), gs_send.at[1], gs_recv.at[1], sibling)
    partner_to_sib.start()

    total = summed[3, pl.ds(x, 1)][0].astype(jnp.float32)
    for dz, dx in plane:
        rs_copy(dz, dx).wait_recv()
        total = total + landed[dz * 4 + dx].astype(jnp.float32)
    y_terms[pl.ds(y, 1)] = total.astype(jnp.bfloat16)[None]

    def y_copy(dy):
        return remote(y_terms.at[y], y_terms.at[y], y_send.at[dy], y_recv.at[dy], at(0, dy, 0))

    for dy in (1, 3, 2):
        y_copy(dy).start()
    for dy in (1, 3, 2):
        y_copy(dy).wait_recv()
    terms = [y_terms[i].astype(jnp.float32) for i in range(SIDE)]
    whole = (terms[0] + terms[1]) + (terms[2] + terms[3])
    c00, c01, c10, c11 = unpack(whole[:HALF], whole[HALF:BS], whole[BS : BS + 1])
    factor = jnp.concatenate(
        [jnp.concatenate([c00, c01], axis=1), jnp.concatenate([c10, c11], axis=1)], axis=0
    )
    block = core * CLASS + z * 4 + x
    mixed, off, diagonal = pack(newton(factor, iters_ref[block]))
    inv_own[:HALF] = mixed.astype(jnp.bfloat16)
    inv_own[HALF:BS] = off.astype(jnp.bfloat16)
    inv_own[BS:] = diagonal.astype(jnp.bfloat16)

    def block_at(dz, dx):
        return core * CLASS + ((z - dz + SIDE) % SIDE) * 4 + (x - dx + SIDE) % SIDE

    def ag_copy(dz, dx):
        slot = dz * 4 + dx
        return remote(inv_own, inv_ref.at[block], ag_send.at[slot], ag_recv.at[slot], at(dx, 0, dz))

    def pass_on(dz, dx):
        slot = dz * 4 + dx
        src = inv_own if slot == 0 else inv_ref.at[block_at(dz, dx)]
        return remote(src, inv_ref.at[block_at(dz, dx)], ags_send.at[slot], ags_recv.at[slot], sibling)

    for dz, dx in plane:
        ag_copy(dz, dx).start()
    pass_on(0, 0).start()
    keep = pltpu.make_async_copy(inv_own, inv_ref.at[block], ag_send.at[0])
    keep.start()

    passed = []
    for i, (dx, dy) in enumerate([(0, 1), (0, 3), (0, 2), (2, 1), (2, 3), (2, 2)]):
        index = dy if dx == 0 else 3 + dy
        came = shard(dx, SIDE - dy)
        arrival = remote(came, came, g_send.at[index], g_recv.at[index], at(0, dy, 0))
        arrival.wait_recv()
        copy = remote(came, came, gs_send.at[2 + i], gs_recv.at[2 + i], sibling)
        copy.start()
        passed.append(copy)

    for dz, dx in plane:
        ag_copy(dz, dx).wait_recv()
        pass_on(dz, dx).start()

    mine.wait()
    keep.wait()
    first_copy.wait_send()
    for copy in g_copies + second_copies:
        copy.wait_send()
    for copy in [own_to_sib, partner_to_sib] + passed:
        copy.wait()
    for k in range(4):
        sib_copy(k).wait_send()
    for dz, dx in plane:
        rs_copy(dz, dx).wait_send()
        ag_copy(dz, dx).wait_send()
        pass_on(dz, dx).wait()
    pass_on(0, 0).wait()
    for dy in (1, 2, 3):
        y_copy(dy).wait_send()


def apply_kernel(inv_ref, grad_ref, out_ref):
    for j in range(inv_ref.shape[0]):
        packed = inv_ref[j].astype(jnp.float32)
        parts = unpack(packed[:HALF], packed[HALF:BS], packed[BS : BS + 1])
        c00, c01, c10, c11 = [part.astype(jnp.bfloat16) for part in parts]
        inverse = jnp.concatenate(
            [jnp.concatenate([c00, c01], axis=1), jnp.concatenate([c10, c11], axis=1)], axis=0
        )
        rows = grad_ref[:, j * BS : (j + 1) * BS]
        out_ref[j * BS : (j + 1) * BS] = lax.dot_general(
            inverse, rows, NT, preferred_element_type=jnp.float32
        ).astype(jnp.bfloat16)


def per_device(activations, gradient, iterations):
    width = activations.shape[1]
    columns = gradient.shape[1] * 16
    anywhere = pl.BlockSpec(memory_space=pl.ANY)
    dma = pltpu.SemaphoreType.DMA
    full, inverses = pl.pallas_call(
        factor_kernel,
        name="factor",
        out_shape=[
            jax.ShapeDtypeStruct((columns, width), jnp.bfloat16),
            jax.ShapeDtypeStruct((BLOCKS, PACK, HALF), jnp.bfloat16),
        ],
        in_specs=[anywhere, anywhere, pl.BlockSpec(memory_space=pltpu.SMEM)],
        out_specs=[anywhere, anywhere],
        scratch_shapes=[
            pltpu.VMEM((8, activations.shape[0], GROUP_COLS), jnp.bfloat16),
            pltpu.VMEM((4, GROUP, PACK, HALF), jnp.bfloat16),
            pltpu.VMEM((4, GROUP, PACK, HALF), jnp.bfloat16),
            pltpu.VMEM((GROUP, PACK, HALF), jnp.float32),
            pltpu.VMEM((4, GROUP, PACK, HALF), jnp.bfloat16),
            pltpu.VMEM((16, PACK, HALF), jnp.bfloat16),
            pltpu.VMEM((SIDE, PACK, HALF), jnp.bfloat16),
            pltpu.VMEM((PACK, HALF), jnp.bfloat16),
            dma((8,)), dma((4,)), dma((4,)), dma((16,)), dma((16,)), dma((4,)), dma((4,)),
            dma((16,)), dma((16,)), dma((16,)), dma((16,)),
            dma, dma((7,)), dma((7,)), dma((8,)), dma((8,)),
        ],
        compiler_params=pltpu.CompilerParams(
            collective_id=0, has_side_effects=True, vmem_limit_bytes=48 << 20
        ),
        cost_estimate=pl.CostEstimate(flops=5 * 10**9, bytes_accessed=32 << 20, transcendentals=0),
    )(activations, gradient.T, iterations)
    step = 4
    return pl.pallas_call(
        apply_kernel,
        name="apply",
        grid=(BLOCKS // step,),
        out_shape=jax.ShapeDtypeStruct((width, columns), jnp.bfloat16),
        in_specs=[
            pl.BlockSpec((step, PACK, HALF), lambda i: (i, 0, 0)),
            pl.BlockSpec((columns, step * BS), lambda i: (0, i)),
        ],
        out_specs=pl.BlockSpec((step * BS, columns), lambda i: (i, 0)),
        compiler_params=pltpu.CompilerParams(vmem_limit_bytes=32 << 20),
        cost_estimate=pl.CostEstimate(flops=2 * 10**9, bytes_accessed=20 << 20, transcendentals=0),
    )(inverses, full)


def solution(mesh):
    placed = (P(("dp", "owner"), None), P(None, ("dp", "owner")), P())
    return jax.shard_map(
        per_device, mesh=mesh, in_specs=placed, out_specs=P(None, "dp"), check_vma=False
    )
```

time: 265 us -> 92.8 us (0.35)
  waiting for transfers between devices: 152 us -> 0 us
  Pallas kernels: 0 us -> 87.5 us
  blocking collectives: 38.7 us -> 0 us
  matrix products: 28.9 us -> 0 us
  between operations: 14.9 us -> 0.02 us
  loops' own time: 9.98 us -> 0 us
  starting transfers between devices: 8.49 us -> 0 us
  local copies, waits for them, and re-layouts: 10.2 us -> 5.07 us
    pallas_call x0 -> x2, Pallas kernels: none -> 87.5 us  [the longest x1 80.7 us: per_device(): pl.pallas_call(factor_kernel, name='factor', out_shape=[jax.ShapeDtypeStr...]
    all_gather x1 -> x0, waiting for transfers between devices: 80.5 us -> none  [per_device(): whole = lax.all_gather(panel, 'owner', axis=0, tiled=True)]
    reduce_scatter x1 -> x0, waiting for transfers between devices: 61.9 us -> none  [per_device(): lax.psum_scatter(partial_value.astype(jnp.bfloat16), 'owner', scatter_dim...]
    psum x1 -> x0, blocking collectives: 38.7 us -> none  [per_device(): factor = lax.psum(factor, 'dp')]
    dot_general x28 -> x0, matrix products: 28.9 us -> none  [the longest x1 14.7 us: per_device(): jnp.einsum('tnb,tnc->nbc', features, features, preferred_element_type=jnp...]
    another operation x2 -> x0, loops' own time: 9.98 us -> none  [newton_inverse(): return lax.fori_loop(0, count, newton, identity / row_bound)]
    all_to_all x1 -> x0, waiting for transfers between devices: 9.78 us -> none  [per_device(): lax.all_to_all(grad_blocks, 'owner', split_axis=0, concat_axis=2, tiled=T...]
    all_to_all x1 -> x0, starting transfers between devices: 8.45 us -> none  [per_device(): lax.all_to_all(grad_blocks, 'owner', split_axis=0, concat_axis=2, tiled=T...]
  transfers between devices with their start and end apart: 3 -> 0, of which waited for: 3 -> 0; matrix products, arithmetic and copies ran while one was open for 1% -> 0% of each run, Pallas kernels for 0% -> 0%
where the time goes in v1:
time: 92.8 us; the launch traced here: 92.6 us
  Pallas kernels  87.5 us (94%)
  local copies, waits for them, and re-layouts  5.07 us (5%)
    pallas_call x1, Pallas kernels, per_device(): pl.pallas_call(factor_kernel, name='factor', out_shape=[jax.ShapeDtypeStr...  80.7 us
    pallas_call x1, Pallas kernels, per_device(): pl.pallas_call(apply_kernel, name='apply', grid=(BLOCKS // step,), out_sh...  6.85 us
    unnamed x6, local copies, waits for them, and re-layouts  5.07 us

profile of v1, /device:TPU:1, one launch (start us, length us, event | category | flops | bytes accessed | tf_op | source)
XLA Modules:
  0.0 92.6 jit_solution(3132235019336662669)
XLA Ops:
  0.0 0.0 copy-start.1
  0.0 1.0 %copy-done.1 = bf16[8192,32]{0,1:T(8,128)(2,1)S(1)} copy-done((bf16[8192,32]{0,1:T(8,128)(2,1)S(1)}, bf16[8192,32]{0,1:T(8,128)(2,1)}, u32[]{:S(2)}) %copy-start.1) | copy-done | bytes 524312
  1.0 0.0 copy-start.2
  1.0 0.7 copy-done.2
  1.7 80.7 %factor.1 = (bf16[512,8192]{1,0:T(8,128)(2,1)}, bf16[32,272,128]{2,1,0:T(8,128)(2,1)S(1)}) custom-call(bf16[1024,8192]{1,0:T(8,128)(2,1)} %act_ref.1, bf16[32,8192]{1,0:T(8,128)(2,1)S(1)} %bitcast.1, s32[32]{0:T(128)S(1)} %copy-done.2), custom_call_target="tpu_custom_call" | custom-call | flops 5000000000 | bytes 33554432 | tf_op jit(solution)/shard_map/factor/pallas_call | solution.py:298
  82.4 0.0 copy-start
  82.4 3.4 %copy-done = bf16[512,8192]{1,0:T(8,128)(2,1)S(1)} copy-done((bf16[512,8192]{1,0:T(8,128)(2,1)S(1)}, bf16[512,8192]{1,0:T(8,128)(2,1)}, u32[]{:S(2)}) %copy-start) | copy-done | bytes 8388632
  85.8 6.8 %apply.1 = bf16[8192,512]{1,0:T(8,128)(2,1)} custom-call(bf16[32,272,128]{2,1,0:T(8,128)(2,1)S(1)} %get-tuple-element.7.inv_ref, bf16[512,8192]{1,0:T(8,128)(2,1)S(1)} %copy-done), custom_call_target="tpu_custom_call" | custom-call | flops 2000000000 | bytes 20971520 | tf_op jit(solution)/shard_map/apply/pallas_call | solution.py:326
Async XLA Ops:
  0.0 1.0 %copy-start.1 = (bf16[8192,32]{0,1:T(8,128)(2,1)S(1)}, bf16[8192,32]{0,1:T(8,128)(2,1)}, u32[]{:S(2)}) copy-start(bf16[8192,32]{0,1:T(8,128)(2,1)} %param.4) | copy-start | bytes 1572868
  1.0 0.7 copy-start.2
  82.4 3.4 %copy-start = (bf16[512,8192]{1,0:T(8,128)(2,1)S(1)}, bf16[512,8192]{1,0:T(8,128)(2,1)}, u32[]{:S(2)}) copy-start(bf16[512,8192]{1,0:T(8,128)(2,1)} %get-tuple-element.8.grad_ref) | copy-start | bytes 25165828

commit v2 on v1

--- a/solution.py
+++ b/solution.py
@@ -11,6 +11,8 @@
 HALF = BS // 2
 BLOCKS = 32
 PACK = BS + 16
+PART = 144
+PACK_INV = 2 * PART
 TOKENS = 131072
 DAMPING = 0.1
 ITERS = 8
@@ -19,6 +21,7 @@
 GROUP = 4
 GROUP_COLS = GROUP * BS
 CLASS = 16
+AHEAD = 3
 MESH = pl.DeviceIdType.MESH
 
 TN = (((0,), (0,)), ((), ()))
@@ -97,10 +100,10 @@
 def factor_kernel(
     act_ref, grad_ref, iters_ref,
     full_ref, inv_ref,
-    act, to_sib, from_sib, own, summed, landed, y_terms, inv_own,
+    act, to_sib, from_sib, own, summed, landed, y_terms, inv_own, count,
     act_sem, sib_send, sib_recv, rs_send, rs_recv, y_send, y_recv,
-    ag_send, ag_recv, ags_send, ags_recv,
-    g_local, g_send, g_recv, gs_send, gs_recv,
+    ag_send, ag_recv, agy_send, agy_recv, ags_send, ags_recv,
+    local_sem, g_send, g_recv, gs_send, gs_recv,
 ):
     x, y, z, core = here()
     sibling = mesh_id(x, y, z, 1 - core)
@@ -116,13 +119,15 @@
         )
 
     def act_copy(slot):
-        side = jnp.where(slot < 4, 1 - core, core)
-        group = side * 4 + (z + slot % 4 + 1) % SIDE
+        side = 1 - core if slot % 2 == 0 else core
+        group = side * 4 + (z + slot // 2 + 1) % SIDE
         cols = pl.ds(pl.multiple_of(group * GROUP_COLS, GROUP_COLS), GROUP_COLS)
         return pltpu.make_async_copy(act_ref.at[:, cols], act.at[slot], act_sem.at[slot])
 
-    for slot in range(8):
+    for slot in range(AHEAD):
         act_copy(slot).start()
+    counts = pltpu.make_async_copy(iters_ref, count, local_sem.at[2])
+    counts.start()
 
     barrier = pltpu.get_barrier_semaphore()
     partners = [sibling] + [at(dx, 0, dz) for dz, dx in plane] + [at(0, dy, 0) for dy in (1, 2, 3)]
@@ -130,27 +135,41 @@
         pl.semaphore_signal(barrier, inc=1, device_id=partner, device_id_type=MESH)
     pl.semaphore_wait(barrier, len(partners))
 
-    def rows_of(dx, dy, side):
-        first = owner_of((x + dx) % SIDE, (y + dy) % SIDE, side) * 32
-        return pl.ds(pl.multiple_of(first, 32), 32)
-
-    def shard(dx, dy, side=core):
-        return full_ref.at[rows_of(dx, dy, side)]
-
-    mine = pltpu.make_async_copy(grad_ref, shard(0, 0), g_local)
+    def rows_of(dx, dy, first, rows):
+        start = owner_of((x + dx) % SIDE, (y + dy) % SIDE, core) * 32 + first
+        return full_ref.at[pl.ds(pl.multiple_of(start, 16), rows)]
+
+    def shard(dx, dy):
+        return rows_of(dx, dy, 0, 32)
+
+    mine = pltpu.make_async_copy(grad_ref, shard(0, 0), local_sem.at[0])
     mine.start()
-    g_copies = []
-    first_copy = remote(grad_ref, shard(0, 0), g_send.at[0], g_recv.at[0], at(2, 0, 0))
-    first_copy.start()
-    for dy in (1, 3, 2):
-        copy = remote(grad_ref, shard(0, 0), g_send.at[dy], g_recv.at[dy], at(0, dy, 0))
-        copy.start()
-        g_copies.append(copy)
-    own_to_sib = remote(grad_ref, shard(0, 0), gs_send.at[0], gs_recv.at[0], sibling)
-    own_to_sib.start()
+
+    def gather_copy(src, dst, index, dx, dy):
+        return remote(src, dst, g_send.at[index], g_recv.at[index], at(dx, dy, 0))
+
+    own_out = [
+        gather_copy(grad_ref, shard(0, 0), 0, 0, 1),
+        gather_copy(grad_ref, shard(0, 0), 1, 0, 3),
+        gather_copy(grad_ref, shard(0, 0), 2, 2, 0),
+    ]
+    for copy in own_out:
+        copy.start()
+
+    def arrived(index, place):
+        gather_copy(place, place, index, 0, 1).wait_recv()
+
+    def sib_shard(index, place, src=None):
+        copy = remote(place if src is None else src, place, gs_send.at[index], gs_recv.at[index], sibling)
+        copy.start()
+        return copy
+
+    to_sibling = [sib_shard(0, shard(0, 0), grad_ref)]
 
     def products(slot, store):
         act_copy(slot).wait()
+        if slot + AHEAD < 8:
+            act_copy(slot + AHEAD).start()
         for j in range(GROUP):
             cols = act[slot, :, j * BS : (j + 1) * BS]
             mixed, off, diagonal = pack(lax.dot_general(cols, cols, TN, preferred_element_type=jnp.float32))
@@ -161,16 +180,6 @@
     def sib_copy(k):
         return remote(to_sib.at[k], from_sib.at[k], sib_send.at[k], sib_recv.at[k], sibling)
 
-    def sibling_group(k, carry):
-        def store(j, first, rows, value):
-            to_sib[k, j, pl.ds(first, rows), :] = value.astype(jnp.bfloat16)
-
-        products(k, store)
-        sib_copy(k).start()
-        return carry
-
-    lax.fori_loop(0, 4, sibling_group, 0)
-
     def rs_copy(dz, dx):
         k = (dz + 3) % 4
         slot = dz * 4 + dx
@@ -178,28 +187,37 @@
             summed.at[k, (x + dx) % SIDE], landed.at[slot], rs_send.at[slot], rs_recv.at[slot], at(dx, 0, dz)
         )
 
-    def own_products(k):
-        def store(j, first, rows, value):
-            own[j, pl.ds(first, rows), :] = value
-
-        products(4 + k, store)
+    for k in range(4):
+
+        def store_sib(j, first, rows, value):
+            to_sib[k, j, first : first + rows] = value.astype(jnp.bfloat16)
+
+        def store_own(j, first, rows, value):
+            own[j, first : first + rows] = value
+
+        products(2 * k, store_sib)
+        sib_copy(k).start()
+        products(2 * k + 1, store_own)
         sib_copy(k).wait_recv()
         summed[k] = (own[...] + from_sib[k].astype(jnp.float32)).astype(jnp.bfloat16)
-
-    for k in range(4):
-        own_products(k)
         for dx in range(SIDE):
             if k < 3 or dx:
                 rs_copy((k + 1) % 4, dx).start()
 
-    first_copy.wait_recv()
-    second_copies = []
-    for dy in (1, 3, 2):
-        copy = remote(shard(2, 0), shard(2, 0), g_send.at[3 + dy], g_recv.at[3 + dy], at(0, dy, 0))
-        copy.start()
-        second_copies.append(copy)
-    partner_to_sib = remote(shard(2, 0), shard(2, 0), gs_send.at[1], gs_recv.at[1], sibling)
-    partner_to_sib.start()
+    arrived(2, shard(2, 0))
+    second = [gather_copy(shard(2, 0), shard(2, 0), 3, 0, 1), gather_copy(shard(2, 0), shard(2, 0), 4, 0, 3)]
+    for copy in second:
+        copy.start()
+    arrived(0, shard(0, 3))
+    arrived(1, shard(0, 1))
+    halves = [
+        gather_copy(rows_of(0, 3, 0, 16), rows_of(0, 3, 0, 16), 5, 0, 1),
+        gather_copy(rows_of(0, 1, 16, 16), rows_of(0, 1, 16, 16), 6, 0, 3),
+    ]
+    for copy in halves:
+        copy.start()
+    second += halves
+    to_sibling += [sib_shard(1, shard(2, 0)), sib_shard(2, shard(0, 3)), sib_shard(3, shard(0, 1))]
 
     total = summed[3, pl.ds(x, 1)][0].astype(jnp.float32)
     for dz, dx in plane:
@@ -221,59 +239,81 @@
         [jnp.concatenate([c00, c01], axis=1), jnp.concatenate([c10, c11], axis=1)], axis=0
     )
     block = core * CLASS + z * 4 + x
-    mixed, off, diagonal = pack(newton(factor, iters_ref[block]))
+    counts.wait()
+    mixed, off, diagonal = pack(newton(factor, count[block]))
     inv_own[:HALF] = mixed.astype(jnp.bfloat16)
     inv_own[HALF:BS] = off.astype(jnp.bfloat16)
-    inv_own[BS:] = diagonal.astype(jnp.bfloat16)
-
-    def block_at(dz, dx):
-        return core * CLASS + ((z - dz + SIDE) % SIDE) * 4 + (x - dx + SIDE) % SIDE
+    inv_own[BS:PACK] = diagonal.astype(jnp.bfloat16)
+    inv_own[PACK:] = jnp.zeros((PACK_INV - PACK, HALF), jnp.bfloat16)
+
+    held = pl.ds(pl.multiple_of((y % 2) * PART, PART), PART)
+    other = pl.ds(pl.multiple_of((1 - y % 2) * PART, PART), PART)
+
+    def place(dz, dx, part):
+        return inv_ref.at[core * CLASS + ((z - dz + SIDE) % SIDE) * 4 + (x - dx + SIDE) % SIDE, part]
 
     def ag_copy(dz, dx):
         slot = dz * 4 + dx
-        return remote(inv_own, inv_ref.at[block], ag_send.at[slot], ag_recv.at[slot], at(dx, 0, dz))
-
-    def pass_on(dz, dx):
+        return remote(inv_own.at[held], place(0, 0, held), ag_send.at[slot], ag_recv.at[slot], at(dx, 0, dz))
+
+    def trade(dz, dx, part):
         slot = dz * 4 + dx
-        src = inv_own if slot == 0 else inv_ref.at[block_at(dz, dx)]
-        return remote(src, inv_ref.at[block_at(dz, dx)], ags_send.at[slot], ags_recv.at[slot], sibling)
+        dy = 1 if dx < 2 else 3
+        return remote(place(dz, dx, part), place(dz, dx, part), agy_send.at[slot], agy_recv.at[slot], at(0, dy, 0))
+
+    def pass_on(dz, dx, part, which):
+        slot = dz * 4 + dx + 16 * which
+        src = inv_own.at[part] if dz == 0 and dx == 0 else place(dz, dx, part)
+        return remote(src, place(dz, dx, part), ags_send.at[slot], ags_recv.at[slot], sibling)
 
     for dz, dx in plane:
         ag_copy(dz, dx).start()
-    pass_on(0, 0).start()
-    keep = pltpu.make_async_copy(inv_own, inv_ref.at[block], ag_send.at[0])
+    whole_rows = pl.ds(0, PACK_INV)
+    pass_on(0, 0, whole_rows, 0).start()
+    keep = pltpu.make_async_copy(inv_own, place(0, 0, whole_rows), local_sem.at[1])
     keep.start()
 
-    passed = []
-    for i, (dx, dy) in enumerate([(0, 1), (0, 3), (0, 2), (2, 1), (2, 3), (2, 2)]):
-        index = dy if dx == 0 else 3 + dy
-        came = shard(dx, SIDE - dy)
-        arrival = remote(came, came, g_send.at[index], g_recv.at[index], at(0, dy, 0))
-        arrival.wait_recv()
-        copy = remote(came, came, gs_send.at[2 + i], gs_recv.at[2 + i], sibling)
-        copy.start()
-        passed.append(copy)
+    arrived(3, shard(2, 3))
+    arrived(4, shard(2, 1))
+    third = [
+        gather_copy(rows_of(2, 3, 0, 16), rows_of(2, 3, 0, 16), 7, 0, 1),
+        gather_copy(rows_of(2, 1, 16, 16), rows_of(2, 1, 16, 16), 8, 0, 3),
+    ]
+    for copy in third:
+        copy.start()
+    to_sibling += [sib_shard(4, shard(2, 3)), sib_shard(5, shard(2, 1))]
+    arrived(5, rows_of(0, 2, 0, 16))
+    arrived(6, rows_of(0, 2, 16, 16))
+    to_sibling += [sib_shard(6, shard(0, 2))]
 
     for dz, dx in plane:
         ag_copy(dz, dx).wait_recv()
-        pass_on(dz, dx).start()
+        trade(dz, dx, held).start()
+        pass_on(dz, dx, held, 0).start()
+    for dz, dx in plane:
+        trade(dz, dx, other).wait_recv()
+        pass_on(dz, dx, other, 1).start()
+    arrived(7, rows_of(2, 2, 0, 16))
+    arrived(8, rows_of(2, 2, 16, 16))
+    to_sibling += [sib_shard(7, shard(2, 2))]
 
     mine.wait()
     keep.wait()
-    first_copy.wait_send()
-    for copy in g_copies + second_copies:
+    for copy in own_out + second + third:
         copy.wait_send()
-    for copy in [own_to_sib, partner_to_sib] + passed:
-        copy.wait()
     for k in range(4):
         sib_copy(k).wait_send()
     for dz, dx in plane:
         rs_copy(dz, dx).wait_send()
         ag_copy(dz, dx).wait_send()
-        pass_on(dz, dx).wait()
-    pass_on(0, 0).wait()
+        trade(dz, dx, held).wait_send()
+        pass_on(dz, dx, held, 0).wait()
+        pass_on(dz, dx, other, 1).wait()
+    pass_on(0, 0, whole_rows, 0).wait()
     for dy in (1, 2, 3):
         y_copy(dy).wait_send()
+    for copy in to_sibling:
+        copy.wait()
 
 
 def apply_kernel(inv_ref, grad_ref, out_ref):
@@ -294,15 +334,16 @@
     width = activations.shape[1]
     columns = gradient.shape[1] * 16
     anywhere = pl.BlockSpec(memory_space=pl.ANY)
+    hbm = pl.BlockSpec(memory_space=pltpu.HBM)
     dma = pltpu.SemaphoreType.DMA
     full, inverses = pl.pallas_call(
         factor_kernel,
         name="factor",
         out_shape=[
             jax.ShapeDtypeStruct((columns, width), jnp.bfloat16),
-            jax.ShapeDtypeStruct((BLOCKS, PACK, HALF), jnp.bfloat16),
+            jax.ShapeDtypeStruct((BLOCKS, PACK_INV, HALF), jnp.bfloat16),
         ],
-        in_specs=[anywhere, anywhere, pl.BlockSpec(memory_space=pltpu.SMEM)],
+        in_specs=[hbm, hbm, hbm],
         out_specs=[anywhere, anywhere],
         scratch_shapes=[
             pltpu.VMEM((8, activations.shape[0], GROUP_COLS), jnp.bfloat16),
@@ -312,13 +353,14 @@
             pltpu.VMEM((4, GROUP, PACK, HALF), jnp.bfloat16),
             pltpu.VMEM((16, PACK, HALF), jnp.bfloat16),
             pltpu.VMEM((SIDE, PACK, HALF), jnp.bfloat16),
-            pltpu.VMEM((PACK, HALF), jnp.bfloat16),
+            pltpu.VMEM((PACK_INV, HALF), jnp.bfloat16),
+            pltpu.SMEM((BLOCKS,), jnp.int32),
             dma((8,)), dma((4,)), dma((4,)), dma((16,)), dma((16,)), dma((4,)), dma((4,)),
-            dma((16,)), dma((16,)), dma((16,)), dma((16,)),
-            dma, dma((7,)), dma((7,)), dma((8,)), dma((8,)),
+            dma((16,)), dma((16,)), dma((16,)), dma((16,)), dma((32,)), dma((32,)),
+            dma((3,)), dma((9,)), dma((9,)), dma((8,)), dma((8,)),
         ],
         compiler_params=pltpu.CompilerParams(
-            collective_id=0, has_side_effects=True, vmem_limit_bytes=48 << 20
+            collective_id=0, has_side_effects=True, vmem_limit_bytes=32 << 20
         ),
         cost_estimate=pl.CostEstimate(flops=5 * 10**9, bytes_accessed=32 << 20, transcendentals=0),
     )(activations, gradient.T, iterations)
@@ -329,7 +371,7 @@
         grid=(BLOCKS // step,),
         out_shape=jax.ShapeDtypeStruct((width, columns), jnp.bfloat16),
         in_specs=[
-            pl.BlockSpec((step, PACK, HALF), lambda i: (i, 0, 0)),
+            pl.BlockSpec((step, PACK_INV, HALF), lambda i: (i, 0, 0)),
             pl.BlockSpec((columns, step * BS), lambda i: (0, i)),
         ],
         out_specs=pl.BlockSpec((step * BS, columns), lambda i: (i, 0)),

time: 92.8 us -> 71.2 us (0.77)
  Pallas kernels: 87.5 us -> 69.4 us
  local copies, waits for them, and re-layouts: 5.07 us -> 1.7 us
    pallas_call x1, Pallas kernels: 80.7 us -> 62.6 us  [per_device(): pl.pallas_call(factor_kernel, name='factor', out_shape=[jax.ShapeDtypeStr...]
    unnamed x6 -> x4, local copies, waits for them, and re-layouts: 5.07 us -> 1.7 us
where the time goes in v2:
time: 71.2 us; the launch traced here: 71.1 us
  Pallas kernels  69.4 us (97%)
  local copies, waits for them, and re-layouts  1.7 us (2%)
    pallas_call x1, Pallas kernels, per_device(): pl.pallas_call(factor_kernel, name='factor', out_shape=[jax.ShapeDtypeStr...  62.6 us
    pallas_call x1, Pallas kernels, per_device(): pl.pallas_call(apply_kernel, name='apply', grid=(BLOCKS // step,), out_sh...  6.79 us
    unnamed x4, local copies, waits for them, and re-layouts  1.7 us

profile of v2, /device:TPU:1, one launch (start us, length us, event | category | flops | bytes accessed | tf_op | source)
XLA Modules:
  0.0 71.1 jit_solution(310032815944770237)
XLA Ops:
  0.0 0.0 copy-start
  0.0 1.0 %copy-done = bf16[8192,32]{0,1:T(8,128)(2,1)S(1)} copy-done((bf16[8192,32]{0,1:T(8,128)(2,1)S(1)}, bf16[8192,32]{0,1:T(8,128)(2,1)}, u32[]{:S(2)}) %copy-start) | copy-done | bytes 524312
  1.0 0.0 copy-start.1
  1.0 0.7 copy-done.1
  1.7 62.6 %factor.1 = (bf16[512,8192]{1,0:T(8,128)(2,1)S(1)}, bf16[32,288,128]{2,1,0:T(8,128)(2,1)S(1)}) custom-call(bf16[1024,8192]{1,0:T(8,128)(2,1)} %act_ref.1, bf16[32,8192]{1,0:T(8,128)(2,1)S(1)} %bitcast.1, s32[32]{0:T(128)S(1)} %copy-done.1), custom_call_target="tpu_custom_call" | custom-call | flops 5000000000 | bytes 33554432 | tf_op jit(solution)/shard_map/factor/pallas_call | solution.py:339
  64.3 6.8 %apply.1 = bf16[8192,512]{1,0:T(8,128)(2,1)} custom-call(bf16[32,288,128]{2,1,0:T(8,128)(2,1)S(1)} %get-tuple-element.7.inv_ref, bf16[512,8192]{1,0:T(8,128)(2,1)S(1)} %get-tuple-element.8.grad_ref), custom_call_target="tpu_custom_call" | custom-call | flops 2000000000 | bytes 20971520 | tf_op jit(solution)/shard_map/apply/pallas_call | solution.py:368
Async XLA Ops:
  0.0 1.0 %copy-start = (bf16[8192,32]{0,1:T(8,128)(2,1)S(1)}, bf16[8192,32]{0,1:T(8,128)(2,1)}, u32[]{:S(2)}) copy-start(bf16[8192,32]{0,1:T(8,128)(2,1)} %param.4) | copy-start | bytes 1572868
  1.0 0.7 copy-start.1

commit v3 on v2

v3 whole, which is shorter than its diff:
```python
import functools

import jax
import jax.numpy as jnp
from jax import lax
from jax.experimental import pallas as pl
from jax.experimental.pallas import tpu as pltpu
from jax.sharding import PartitionSpec as P

BS = 256
HALF = BS // 2
BLOCKS = 32
PACK = BS + 16
PART = 144
PACK_INV = 2 * PART
TOKENS = 131072
DAMPING = 0.1
ITERS = 8
LEAST_ITERS = 5
SIDE = 4
GROUP = 4
GROUP_COLS = GROUP * BS
CLASS = 16
AHEAD = 4
AWAY = (2, 1, 3, 0)
X_EARLY = 4096
Y_EARLY = 2048
ACROSS = 4096
S2_FIRST = False
MESH = pl.DeviceIdType.MESH

TN = (((0,), (0,)), ((), ()))
NT = (((1,), (1,)), ((), ()))


def here():
    shard = lax.axis_index("dp")
    owner = lax.axis_index("owner")
    x = (owner // 8) * 2 + shard % 2
    return x, (owner // 2) % 4, shard // 2, owner % 2


def mesh_id(x, y, z, core):
    return (z * 2 + x % 2, (x // 2) * 8 + y * 2 + core)


def owner_of(x, y, core):
    return (x // 2) * 8 + y * 2 + core


def tile_iota():
    rows = lax.broadcasted_iota(jnp.int32, (HALF, HALF), 0)
    cols = lax.broadcasted_iota(jnp.int32, (HALF, HALF), 1)
    return rows, cols


def pack(block):
    rows, cols = tile_iota()
    low = block[HALF:, HALF:]
    mixed = jnp.where(rows <= cols, block[:HALF, :HALF], low)
    diagonal = jnp.sum(jnp.where(rows == cols, low, 0.0), axis=0, keepdims=True)
    return mixed, block[:HALF, HALF:], jnp.broadcast_to(diagonal, (16, HALF))


def unpack(mixed, off, diagonal):
    rows, cols = tile_iota()
    turned = mixed.T
    first = jnp.where(rows <= cols, mixed, turned)
    second = jnp.where(rows > cols, mixed, jnp.where(rows < cols, turned, diagonal))
    return first, off, off.T, second


def split(value):
    high = value.astype(jnp.bfloat16)
    return high, (value - high.astype(jnp.float32)).astype(jnp.bfloat16)


def dot3(left, right):
    lh, ll = split(left)
    rh, rl = split(right)
    mul = functools.partial(jnp.dot, preferred_element_type=jnp.float32)
    return mul(lh, rh) + (mul(lh, rl) + mul(ll, rh))


def newton(factor, count):
    rows = lax.broadcasted_iota(jnp.int32, (BS, BS), 0)
    cols = lax.broadcasted_iota(jnp.int32, (BS, BS), 1)
    identity = jnp.where(rows == cols, 1.0, 0.0)
    damped = factor / TOKENS + DAMPING * identity
    bound = jnp.max(jnp.sum(jnp.abs(damped), axis=1))
    ratio = damped / bound
    approx = (2.0 * identity - ratio) / bound
    ratio = 2.0 * ratio - dot3(ratio, ratio)
    for step in range(1, ITERS):
        if step < ITERS - 1:
            both = dot3(jnp.concatenate([ratio, approx], axis=0), ratio)
            later = 2.0 * approx - both[BS:]
            ratio = 2.0 * ratio - both[:BS]
        else:
            later = 2.0 * approx - dot3(approx, ratio)
        approx = later if step < LEAST_ITERS else jnp.where(step < count, later, approx)
    return approx


def factor_kernel(
    act_ref, grad_ref, iters_ref,
    full_ref, inv_ref,
    act, to_sib, from_sib, own, summed, z_land, x_land, x_terms, z_terms, x_last, z_last, y_terms, inv_own, count,
    act_sem, sib_send, sib_recv, z_send, z_recv, x_send, x_recv, y_send, y_recv, x2_send, x2_recv, z2_send, z2_recv,
    agx_send, agx_recv, agz_send, agz_recv, agx2_send, agx2_recv, agz2_send, agz2_recv, ags_send, ags_recv,
    local_sem, g_send, g_recv, gs_send, gs_recv,
):
    x, y, z, core = here()
    sibling = mesh_id(x, y, z, 1 - core)

    def at(dx, dy, dz):
        return mesh_id((x + dx) % SIDE, (y + dy) % SIDE, (z + dz) % SIDE, core)

    def remote(src, dst, send, recv, target):
        return pltpu.make_async_remote_copy(
            src_ref=src, dst_ref=dst, send_sem=send, recv_sem=recv, device_id=target, device_id_type=MESH
        )

    work = [("sib", 0), ("sib", 1), ("own", 0), ("sib", 2), ("own", 1), ("sib", 3), ("own", 2), ("own", 3)]

    def act_copy(slot):
        kind, k = work[slot]
        side = 1 - core if kind == "sib" else core
        group = side * 4 + (z + AWAY[k]) % SIDE
        cols = pl.ds(pl.multiple_of(group * GROUP_COLS, GROUP_COLS), GROUP_COLS)
        return pltpu.make_async_copy(act_ref.at[:, cols], act.at[slot], act_sem.at[slot])

    for slot in range(AHEAD):
        act_copy(slot).start()
    counts = pltpu.make_async_copy(iters_ref, count, local_sem.at[2])
    counts.start()

    barrier = pltpu.get_barrier_semaphore()
    partners = [sibling]
    for d in (1, 2, 3):
        partners += [at(0, d, 0), at(d, 0, 0), at(0, 0, d)]
    for partner in partners:
        pl.semaphore_signal(barrier, inc=1, device_id=partner, device_id_type=MESH)

    def products(slot, store):
        act_copy(slot).wait()
        if slot + AHEAD < 8:
            act_copy(slot + AHEAD).start()
        for j in range(GROUP):
            cols = act[slot, :, j * BS : (j + 1) * BS]
            mixed, off, diagonal = pack(lax.dot_general(cols, cols, TN, preferred_element_type=jnp.float32))
            store(j, 0, HALF, mixed)
            store(j, HALF, HALF, off)
            store(j, BS, 16, diagonal)

    def sib_products(slot):
        k = work[slot][1]

        def store(j, first, rows, value):
            to_sib[k, j, first : first + rows] = value.astype(jnp.bfloat16)

        products(slot, store)

    sib_products(0)
    pl.semaphore_wait(barrier, len(partners))

    def rows_of(dx, dy, first, rows, cols=slice(None)):
        start = owner_of((x + dx) % SIDE, (y + dy) % SIDE, core) * 32 + first
        return full_ref.at[pl.ds(pl.multiple_of(start, 16), rows), cols]

    def shard(dx, dy):
        return rows_of(dx, dy, 0, 32)

    mine = pltpu.make_async_copy(grad_ref, shard(0, 0), local_sem.at[0])
    mine.start()
    gathers = []

    def gather(index, dx, dy, place, src=None):
        copy = remote(place if src is None else src, place, g_send.at[index], g_recv.at[index], at(dx, dy, 0))
        copy.start()
        gathers.append(copy)

    def arrived(index, place):
        remote(place, place, g_send.at[index], g_recv.at[index], at(0, 1, 0)).wait_recv()

    passes = []

    def to_sibling(index, place, src=None):
        copy = remote(place if src is None else src, place, gs_send.at[index], gs_recv.at[index], sibling)
        copy.start()
        passes.append(copy)

    def columns(first, last):
        return pl.ds(first, last - first)

    def send_parts(index, dx, dy, first, last, src=None):
        cols = columns(first, last)
        gather(index, dx, dy, rows_of(0, 0, 0, 32, cols) if src is None else src, grad_ref.at[:, cols] if src is None else None)

    width = grad_ref.shape[1]
    gather(0, 0, 1, shard(0, 0), grad_ref)
    gather(1, 0, 3, shard(0, 0), grad_ref)
    send_parts(2, 2, 0, 0, X_EARLY)

    def sib_copy(k):
        return remote(to_sib.at[k], from_sib.at[k], sib_send.at[k], sib_recv.at[k], sibling)

    def z_copy(k):
        return remote(summed.at[k, :, :PART], z_land.at[k], z_send.at[k], z_recv.at[k], at(0, 0, AWAY[k]))

    def x_copy(dx, k):
        return remote(
            summed.at[k : k + 2, (x + dx) % SIDE, PART:], x_land.at[dx, k : k + 2],
            x_send.at[dx, k // 2], x_recv.at[dx, k // 2], at(dx, 0, 0),
        )

    sib_copy(0).start()
    for slot in range(1, 8):
        kind, k = work[slot]
        if kind == "sib":
            sib_products(slot)
            sib_copy(k).start()
            continue

        def store_own(j, first, rows, value):
            own[j, first : first + rows] = value

        products(slot, store_own)
        sib_copy(k).wait_recv()
        summed[k] = (own[...] + from_sib[k].astype(jnp.float32)).astype(jnp.bfloat16)
        if k < 3:
            z_copy(k).start()
        if k % 2:
            for dx in (2, 1, 3):
                x_copy(dx, k - 1).start()

    to_sibling(0, shard(0, 0), grad_ref)

    totals = own[:, :PART] + from_sib[3, :, :PART].astype(jnp.float32)
    for k in range(3):
        z_copy(k).wait_recv()
        totals = totals + z_land[k].astype(jnp.float32)
    x_terms[...] = totals.astype(jnp.bfloat16)

    def x_copy2(dx):
        return remote(x_terms.at[(x + dx) % SIDE], x_last.at[dx], x2_send.at[dx], x2_recv.at[dx], at(dx, 0, 0))

    def z_copy2(k):
        return remote(z_terms.at[k], z_last.at[k], z2_send.at[k], z2_recv.at[k], at(0, 0, AWAY[k]))

    for dx in (2, 1, 3):
        x_copy2(dx).start()
    for half in (0, 2):
        for dx in (1, 3, 2):
            x_copy(dx, half).wait_recv()
        for k in (half, half + 1):
            mine_here = summed[k, pl.ds(x, 1), PART:][0].astype(jnp.float32)
            for dx in (1, 3, 2):
                mine_here = mine_here + x_land[dx, k].astype(jnp.float32)
            z_terms[k] = mine_here.astype(jnp.bfloat16)
            if k < 3:
                z_copy2(k).start()

    if X_EARLY < width:
        send_parts(3, 2, 0, X_EARLY, width)
    arrived(2, rows_of(2, 0, 0, 32, columns(0, X_EARLY)))
    if Y_EARLY:
        send_parts(4, 0, 1, 0, Y_EARLY, rows_of(2, 0, 0, 32, columns(0, Y_EARLY)))
        send_parts(5, 0, 3, 0, Y_EARLY, rows_of(2, 0, 0, 32, columns(0, Y_EARLY)))

    first = x_terms[pl.ds(x, 1)][0].astype(jnp.float32)
    for dx in (1, 3, 2):
        x_copy2(dx).wait_recv()
        first = first + x_last[dx].astype(jnp.float32)
    rest = z_terms[3].astype(jnp.float32)
    for k in (1, 2, 0):
        z_copy2(k).wait_recv()
        rest = rest + z_last[k].astype(jnp.float32)
    y_terms[pl.ds(y, 1), :PART] = first.astype(jnp.bfloat16)[None]
    y_terms[pl.ds(y, 1), PART:] = rest.astype(jnp.bfloat16)[None]

    def y_copy(dy):
        return remote(y_terms.at[y], y_terms.at[y], y_send.at[dy], y_recv.at[dy], at(0, dy, 0))

    def send_opposite():
        arrived(6, rows_of(0, 2, 0, 16))
        arrived(7, rows_of(0, 2, 16, 16))
        if ACROSS:
            gather(10, 2, 0, rows_of(0, 2, 0, 32, columns(0, ACROSS)))
        to_sibling(4, shard(0, 2))

    for dy in (2, 1, 3):
        y_copy(dy).start()

    arrived(0, shard(0, 3))
    gather(6, 0, 1, rows_of(0, 3, 0, 16))
    arrived(1, shard(0, 1))
    gather(7, 0, 3, rows_of(0, 1, 16, 16))
    to_sibling(1, shard(0, 3))
    to_sibling(2, shard(0, 1))
    for dy in (1, 3, 2):
        y_copy(dy).wait_recv()

    if X_EARLY < width:
        arrived(3, rows_of(2, 0, 0, 32, columns(X_EARLY, width)))
    send_parts(8, 0, 1, Y_EARLY, width, rows_of(2, 0, 0, 32, columns(Y_EARLY, width)))
    send_parts(9, 0, 3, Y_EARLY, width, rows_of(2, 0, 0, 32, columns(Y_EARLY, width)))
    to_sibling(3, shard(2, 0))
    if S2_FIRST:
        send_opposite()

    terms = [y_terms[i].astype(jnp.float32) for i in range(SIDE)]
    whole = (terms[0] + terms[1]) + (terms[2] + terms[3])
    c00, c01, c10, c11 = unpack(whole[:HALF], whole[HALF:BS], whole[BS : BS + 1])
    factor = jnp.concatenate(
        [jnp.concatenate([c00, c01], axis=1), jnp.concatenate([c10, c11], axis=1)], axis=0
    )
    block = core * CLASS + z * 4 + x
    counts.wait()
    mixed, off, diagonal = pack(newton(factor, count[block]))
    inv_own[:HALF] = mixed.astype(jnp.bfloat16)
    inv_own[HALF:BS] = off.astype(jnp.bfloat16)
    inv_own[BS:PACK] = diagonal.astype(jnp.bfloat16)
    inv_own[PACK:] = jnp.zeros((PACK_INV - PACK, HALF), jnp.bfloat16)

    upper, lower = pl.ds(0, PART), pl.ds(PART, PART)

    def agx_copy(d):
        return remote(inv_own.at[upper], inv_ref.at[core, z, x, upper], agx_send.at[d], agx_recv.at[d], at(d, 0, 0))

    def agz_copy(d):
        return remote(inv_own.at[lower], inv_ref.at[core, z, x, lower], agz_send.at[d], agz_recv.at[d], at(0, 0, d))

    def along_x(d):
        return inv_ref.at[core, (z + SIDE - d) % SIDE, :, upper]

    def along_z(d):
        return inv_ref.at[core, :, (x + SIDE - d) % SIDE, lower]

    def agz_copy2(d):
        return remote(along_x(0), along_x(0), agz2_send.at[d], agz2_recv.at[d], at(0, 0, d))

    def agx_copy2(d):
        return remote(along_z(0), along_z(0), agx2_send.at[d], agx2_recv.at[d], at(d, 0, 0))

    def pass_on(place, slot):
        return remote(place, place, ags_send.at[slot], ags_recv.at[slot], sibling)

    for d in (2, 1, 3):
        agx_copy(d).start()
        agz_copy(d).start()
    keep = pltpu.make_async_copy(inv_own, inv_ref.at[core, z, x], local_sem.at[1])
    keep.start()
    keep.wait()
    for d in (1, 3, 2):
        agx_copy(d).wait_recv()
    for d in (2, 1, 3):
        agz_copy2(d).start()
    for d in (1, 3, 2):
        agz_copy(d).wait_recv()
    for d in (2, 1, 3):
        agx_copy2(d).start()
    pass_on(along_x(0), 0).start()
    pass_on(along_z(0), 4).start()
    if not S2_FIRST:
        send_opposite()
    for dy, one, two in ((3, 4, 8), (1, 5, 9)):
        if Y_EARLY:
            arrived(one, rows_of(2, dy, 0, 32, columns(0, Y_EARLY)))
        arrived(two, rows_of(2, dy, 0, 32, columns(Y_EARLY, width)))
        if ACROSS < width:
            first_row = 0 if dy == 3 else 16
            gather(11 + first_row // 16, 0, 4 - dy, rows_of(2, dy, first_row, 16, columns(ACROSS, width)))
        to_sibling(5 + first_row // 16 if ACROSS < width else 5 + dy // 2, shard(2, dy))
    for d in (1, 3, 2):
        agz_copy2(d).wait_recv()
        pass_on(along_x(d), d).start()
        agx_copy2(d).wait_recv()
        pass_on(along_z(d), 4 + d).start()
    if ACROSS:
        arrived(10, rows_of(2, 2, 0, 32, columns(0, ACROSS)))
    if ACROSS < width:
        arrived(11, rows_of(2, 2, 0, 16, columns(ACROSS, width)))
        arrived(12, rows_of(2, 2, 16, 16, columns(ACROSS, width)))
    to_sibling(7, shard(2, 2))

    mine.wait()
    for copy in gathers:
        copy.wait_send()
    for k in range(4):
        sib_copy(k).wait_send()
    for k in range(3):
        z_copy(k).wait_send()
        z_copy2(k).wait_send()
    for d in (1, 2, 3):
        x_copy(d, 0).wait_send()
        x_copy(d, 2).wait_send()
        x_copy2(d).wait_send()
        y_copy(d).wait_send()
        agx_copy(d).wait_send()
        agz_copy(d).wait_send()
        agx_copy2(d).wait_send()
        agz_copy2(d).wait_send()
    for d in range(4):
        pass_on(along_x(d), d).wait()
        pass_on(along_z(d), 4 + d).wait()
    for copy in passes:
        copy.wait()


def apply_kernel(inv_ref, grad_ref, out_ref):
    for j in range(inv_ref.shape[0]):
        packed = inv_ref[j].astype(jnp.float32)
        parts = unpack(packed[:HALF], packed[HALF:BS], packed[BS : BS + 1])
        c00, c01, c10, c11 = [part.astype(jnp.bfloat16) for part in parts]
        inverse = jnp.concatenate(
            [jnp.concatenate([c00, c01], axis=1), jnp.concatenate([c10, c11], axis=1)], axis=0
        )
        rows = grad_ref[:, j * BS : (j + 1) * BS]
        out_ref[j * BS : (j + 1) * BS] = lax.dot_general(
            inverse, rows, NT, preferred_element_type=jnp.float32
        ).astype(jnp.bfloat16)


def per_device(activations, gradient, iterations):
    width = activations.shape[1]
    columns = gradient.shape[1] * 16
    anywhere = pl.BlockSpec(memory_space=pl.ANY)
    hbm = pl.BlockSpec(memory_space=pltpu.HBM)
    dma = pltpu.SemaphoreType.DMA
    full, inverses = pl.pallas_call(
        factor_kernel,
        name="factor",
        out_shape=[
            jax.ShapeDtypeStruct((columns, width), jnp.bfloat16),
            jax.ShapeDtypeStruct((2, SIDE, SIDE, PACK_INV, HALF), jnp.bfloat16),
        ],
        in_specs=[hbm, hbm, hbm],
        out_specs=[anywhere, anywhere],
        scratch_shapes=[
            pltpu.VMEM((8, activations.shape[0], GROUP_COLS), jnp.bfloat16),
            pltpu.VMEM((4, GROUP, PACK, HALF), jnp.bfloat16),
            pltpu.VMEM((4, GROUP, PACK, HALF), jnp.bfloat16),
            pltpu.VMEM((GROUP, PACK, HALF), jnp.float32),
            pltpu.VMEM((4, GROUP, PACK, HALF), jnp.bfloat16),
            pltpu.VMEM((3, GROUP, PART, HALF), jnp.bfloat16),
            pltpu.VMEM((SIDE, 4, PACK - PART, HALF), jnp.bfloat16),
            pltpu.VMEM((GROUP, PART, HALF), jnp.bfloat16),
            pltpu.VMEM((4, PACK - PART, HALF), jnp.bfloat16),
            pltpu.VMEM((SIDE, PART, HALF), jnp.bfloat16),
            pltpu.VMEM((3, PACK - PART, HALF), jnp.bfloat16),
            pltpu.VMEM((SIDE, PACK, HALF), jnp.bfloat16),
            pltpu.VMEM((PACK_INV, HALF), jnp.bfloat16),
            pltpu.SMEM((BLOCKS,), jnp.int32),
            dma((8,)), dma((4,)), dma((4,)), dma((3,)), dma((3,)), dma((4, 2)), dma((4, 2)), dma((4,)), dma((4,)),
            dma((4,)), dma((4,)), dma((3,)), dma((3,)),
            dma((4,)), dma((4,)), dma((4,)), dma((4,)), dma((4,)), dma((4,)), dma((4,)), dma((4,)), dma((8,)), dma((8,)),
            dma((3,)), dma((13,)), dma((13,)), dma((8,)), dma((8,)),
        ],
        compiler_params=pltpu.CompilerParams(
            collective_id=0, has_side_effects=True, vmem_limit_bytes=32 << 20
        ),
        cost_estimate=pl.CostEstimate(flops=5 * 10**9, bytes_accessed=32 << 20, transcendentals=0),
    )(activations, gradient.T, iterations)
    step = 8
    return pl.pallas_call(
        apply_kernel,
        name="apply",
        grid=(BLOCKS // step,),
        out_shape=jax.ShapeDtypeStruct((width, columns), jnp.bfloat16),
        in_specs=[
            pl.BlockSpec((step, PACK_INV, HALF), lambda i: (i, 0, 0)),
            pl.BlockSpec((columns, step * BS), lambda i: (0, i)),
        ],
        out_specs=pl.BlockSpec((step * BS, columns), lambda i: (i, 0)),
        compiler_params=pltpu.CompilerParams(vmem_limit_bytes=32 << 20),
        cost_estimate=pl.CostEstimate(flops=2 * 10**9, bytes_accessed=20 << 20, transcendentals=0),
    )(inverses.reshape(BLOCKS, PACK_INV, HALF), full)


def solution(mesh):
    placed = (P(("dp", "owner"), None), P(None, ("dp", "owner")), P())
    return jax.shard_map(
        per_device, mesh=mesh, in_specs=placed, out_specs=P(None, "dp"), check_vma=False
    )
```

time: 71.2 us -> 61.7 us (0.87)
  Pallas kernels: 69.4 us -> 59.8 us
    pallas_call x1, Pallas kernels: 62.6 us -> 54.4 us  [per_device(): pl.pallas_call(factor_kernel, name='factor', out_shape=[jax.ShapeDtypeStr...]
    pallas_call x1, Pallas kernels: 6.79 us -> 5.43 us  [per_device(): pl.pallas_call(apply_kernel, name='apply', grid=(BLOCKS // step,), out_sh...]
where the time goes in v3:
time: 61.7 us; the launch traced here: 61.5 us
  Pallas kernels  59.8 us (97%)
  local copies, waits for them, and re-layouts  1.7 us (3%)
    pallas_call x1, Pallas kernels, per_device(): pl.pallas_call(factor_kernel, name='factor', out_shape=[jax.ShapeDtypeStr...  54.4 us
    pallas_call x1, Pallas kernels, per_device(): pl.pallas_call(apply_kernel, name='apply', grid=(BLOCKS // step,), out_sh...  5.43 us
    unnamed x4, local copies, waits for them, and re-layouts  1.7 us

profile of v3, /device:TPU:1, one launch (start us, length us, event | category | flops | bytes accessed | tf_op | source)
XLA Modules:
  0.0 61.5 jit_solution(7047100342532499408)
XLA Ops:
  0.0 0.0 copy-start
  0.0 1.0 %copy-done = bf16[8192,32]{0,1:T(8,128)(2,1)S(1)} copy-done((bf16[8192,32]{0,1:T(8,128)(2,1)S(1)}, bf16[8192,32]{0,1:T(8,128)(2,1)}, u32[]{:S(2)}) %copy-start) | copy-done | bytes 524312
  1.0 0.0 copy-start.1
  1.0 0.7 %copy-done.1 = s32[32]{0:T(128)S(1)} copy-done((s32[32]{0:T(128)S(1)}, s32[32]{0:T(128)}, u32[]{:S(2)}) %copy-start.1) | copy-done | bytes 152
  1.7 54.4 %factor.1 = (bf16[512,8192]{1,0:T(8,128)(2,1)S(1)}, bf16[2,4,4,288,128]{4,3,2,1,0:T(8,128)(2,1)S(1)}) custom-call(bf16[1024,8192]{1,0:T(8,128)(2,1)} %act_ref.1, bf16[32,8192]{1,0:T(8,128)(2,1)S(1)} %bitcast.3, s32[32]{0:T(128)S(1)} %copy-done.1), custom_call_target="tpu_custom_call" | custom-call | flops 5000000000 | bytes 33554432 | tf_op jit(solution)/shard_map/factor/pallas_call | solution.py:431
  56.1 5.4 %apply.1 = bf16[8192,512]{1,0:T(8,128)(2,1)} custom-call(bf16[32,288,128]{2,1,0:T(8,128)(2,1)S(1)} %bitcast.2, bf16[512,8192]{1,0:T(8,128)(2,1)S(1)} %get-tuple-element.8.grad_ref), custom_call_target="tpu_custom_call" | custom-call | flops 2000000000 | bytes 20971520 | tf_op jit(solution)/shard_map/apply/pallas_call | solution.py:466
Async XLA Ops:
  0.0 1.0 %copy-start = (bf16[8192,32]{0,1:T(8,128)(2,1)S(1)}, bf16[8192,32]{0,1:T(8,128)(2,1)}, u32[]{:S(2)}) copy-start(bf16[8192,32]{0,1:T(8,128)(2,1)} %param.4) | copy-start | bytes 1572868
  1.0 0.7 %copy-start.1 = (s32[32]{0:T(128)S(1)}, s32[32]{0:T(128)}, u32[]{:S(2)}) copy-start(s32[32]{0:T(128)} %iters_ref.1) | copy-start | bytes 388

commit v4 on v3

--- a/solution.py
+++ b/solution.py
@@ -21,11 +21,12 @@
 GROUP = 4
 GROUP_COLS = GROUP * BS
 CLASS = 16
+WRITE = 4
 AHEAD = 4
 AWAY = (2, 1, 3, 0)
 X_EARLY = 4096
 Y_EARLY = 2048
-ACROSS = 4096
+ACROSS = 2048
 S2_FIRST = False
 MESH = pl.DeviceIdType.MESH
 
@@ -408,18 +409,27 @@
         copy.wait()
 
 
-def apply_kernel(inv_ref, grad_ref, out_ref):
-    for j in range(inv_ref.shape[0]):
-        packed = inv_ref[j].astype(jnp.float32)
+def apply_kernel(inv_ref, grad_ref, out_ref, stage, sem):
+    def block_copy(b):
+        rows = pl.ds(b * BS, BS)
+        return pltpu.make_async_copy(stage.at[rows], out_ref.at[rows], sem.at[b])
+
+    for b in range(BLOCKS):
+        packed = inv_ref[b].astype(jnp.float32)
         parts = unpack(packed[:HALF], packed[HALF:BS], packed[BS : BS + 1])
         c00, c01, c10, c11 = [part.astype(jnp.bfloat16) for part in parts]
         inverse = jnp.concatenate(
             [jnp.concatenate([c00, c01], axis=1), jnp.concatenate([c10, c11], axis=1)], axis=0
         )
-        rows = grad_ref[:, j * BS : (j + 1) * BS]
-        out_ref[j * BS : (j + 1) * BS] = lax.dot_general(
+        rows = grad_ref[:, b * BS : (b + 1) * BS]
+        stage[b * BS : (b + 1) * BS] = lax.dot_general(
             inverse, rows, NT, preferred_element_type=jnp.float32
         ).astype(jnp.bfloat16)
+        if b % WRITE == WRITE - 1:
+            for w in range(b - WRITE + 1, b + 1):
+                block_copy(w).start()
+    for b in range(BLOCKS):
+        block_copy(b).wait()
 
 
 def per_device(activations, gradient, iterations):
@@ -461,18 +471,15 @@
             collective_id=0, has_side_effects=True, vmem_limit_bytes=32 << 20
         ),
         cost_estimate=pl.CostEstimate(flops=5 * 10**9, bytes_accessed=32 << 20, transcendentals=0),
-    )(activations, gradient.T, iterations)
-    step = 8
+    )(activations, pltpu.with_memory_space_constraint(gradient.T, pltpu.HBM), pltpu.with_memory_space_constraint(iterations, pltpu.HBM))
+    vmem = pl.BlockSpec(memory_space=pltpu.VMEM)
     return pl.pallas_call(
         apply_kernel,
         name="apply",
-        grid=(BLOCKS // step,),
         out_shape=jax.ShapeDtypeStruct((width, columns), jnp.bfloat16),
-        in_specs=[
-            pl.BlockSpec((step, PACK_INV, HALF), lambda i: (i, 0, 0)),
-            pl.BlockSpec((columns, step * BS), lambda i: (0, i)),
-        ],
-        out_specs=pl.BlockSpec((step * BS, columns), lambda i: (i, 0)),
+        in_specs=[vmem, vmem],
+        out_specs=pl.BlockSpec(memory_space=pltpu.HBM),
+        scratch_shapes=[pltpu.VMEM((width, columns), jnp.bfloat16), dma((BLOCKS,))],
         compiler_params=pltpu.CompilerParams(vmem_limit_bytes=32 << 20),
         cost_estimate=pl.CostEstimate(flops=2 * 10**9, bytes_accessed=20 << 20, transcendentals=0),
     )(inverses.reshape(BLOCKS, PACK_INV, HALF), full)

time: 61.7 us -> 56.5 us (0.916)
  Pallas kernels: 59.8 us -> 56.4 us
  local copies, waits for them, and re-layouts: 1.7 us -> 0 us
    pallas_call x1, Pallas kernels: 54.4 us -> 52.3 us  [per_device(): pl.pallas_call(factor_kernel, name='factor', out_shape=[jax.ShapeDtypeStr...]
    unnamed x4 -> x0, local copies, waits for them, and re-layouts: 1.7 us -> none
    pallas_call x1, Pallas kernels: 5.43 us -> 4.03 us  [per_device(): pl.pallas_call(apply_kernel, name='apply', out_shape=jax.ShapeDtypeStruct...]
where the time goes in v4:
time: 56.5 us; the launch traced here: 56.4 us
  Pallas kernels  56.4 us (100%)
    pallas_call x1, Pallas kernels, per_device(): pl.pallas_call(factor_kernel, name='factor', out_shape=[jax.ShapeDtypeStr...  52.3 us
    pallas_call x1, Pallas kernels, per_device(): pl.pallas_call(apply_kernel, name='apply', out_shape=jax.ShapeDtypeStruct...  4.03 us

profile of v4, /device:TPU:1, one launch (start us, length us, event | category | flops | bytes accessed | tf_op | source)
XLA Modules:
  0.0 56.4 jit_solution(16491522991706393278)
XLA Ops:
  0.0 52.3 %factor.1 = (bf16[512,8192]{1,0:T(8,128)(2,1)S(1)}, bf16[2,4,4,288,128]{4,3,2,1,0:T(8,128)(2,1)S(1)}) custom-call(bf16[1024,8192]{1,0:T(8,128)(2,1)} %act_ref.1, bf16[32,8192]{1,0:T(8,128)(2,1)} %bitcast.3, s32[32]{0:T(128)} %iters_ref.1), custom_call_target="tpu_custom_call" | custom-call | flops 5000000000 | bytes 33554432 | tf_op jit(solution)/shard_map/factor/pallas_call | solution.py:441
  52.3 4.0 %apply.1 = bf16[8192,512]{1,0:T(8,128)(2,1)} custom-call(bf16[32,288,128]{2,1,0:T(8,128)(2,1)S(1)} %bitcast.2, bf16[512,8192]{1,0:T(8,128)(2,1)S(1)} %get-tuple-element.8.grad_ref), custom_call_target="tpu_custom_call" | custom-call | flops 2000000000 | bytes 20971520 | tf_op jit(solution)/shard_map/apply/pallas_call | solution.py:476

commit v5 on v4

--- a/solution.py
+++ b/solution.py
@@ -24,10 +24,9 @@
 WRITE = 4
 AHEAD = 4
 AWAY = (2, 1, 3, 0)
-X_EARLY = 4096
+X_EARLY = 3072
 Y_EARLY = 2048
 ACROSS = 2048
-S2_FIRST = False
 MESH = pl.DeviceIdType.MESH
 
 TN = (((0,), (0,)), ((), ()))
@@ -262,8 +261,6 @@
             if k < 3:
                 z_copy2(k).start()
 
-    if X_EARLY < width:
-        send_parts(3, 2, 0, X_EARLY, width)
     arrived(2, rows_of(2, 0, 0, 32, columns(0, X_EARLY)))
     if Y_EARLY:
         send_parts(4, 0, 1, 0, Y_EARLY, rows_of(2, 0, 0, 32, columns(0, Y_EARLY)))
@@ -293,6 +290,8 @@
     for dy in (2, 1, 3):
         y_copy(dy).start()
 
+    if X_EARLY < width:
+        send_parts(3, 2, 0, X_EARLY, width)
     arrived(0, shard(0, 3))
     gather(6, 0, 1, rows_of(0, 3, 0, 16))
     arrived(1, shard(0, 1))
@@ -301,14 +300,6 @@
     to_sibling(2, shard(0, 1))
     for dy in (1, 3, 2):
         y_copy(dy).wait_recv()
-
-    if X_EARLY < width:
-        arrived(3, rows_of(2, 0, 0, 32, columns(X_EARLY, width)))
-    send_parts(8, 0, 1, Y_EARLY, width, rows_of(2, 0, 0, 32, columns(Y_EARLY, width)))
-    send_parts(9, 0, 3, Y_EARLY, width, rows_of(2, 0, 0, 32, columns(Y_EARLY, width)))
-    to_sibling(3, shard(2, 0))
-    if S2_FIRST:
-        send_opposite()
 
     terms = [y_terms[i].astype(jnp.float32) for i in range(SIDE)]
     whole = (terms[0] + terms[1]) + (terms[2] + terms[3])
@@ -352,6 +343,12 @@
         agz_copy(d).start()
     keep = pltpu.make_async_copy(inv_own, inv_ref.at[core, z, x], local_sem.at[1])
     keep.start()
+
+    if X_EARLY < width:
+        arrived(3, rows_of(2, 0, 0, 32, columns(X_EARLY, width)))
+    send_parts(8, 0, 1, Y_EARLY, width, rows_of(2, 0, 0, 32, columns(Y_EARLY, width)))
+    send_parts(9, 0, 3, Y_EARLY, width, rows_of(2, 0, 0, 32, columns(Y_EARLY, width)))
+    to_sibling(3, shard(2, 0))
     keep.wait()
     for d in (1, 3, 2):
         agx_copy(d).wait_recv()
@@ -363,8 +360,7 @@
         agx_copy2(d).start()
     pass_on(along_x(0), 0).start()
     pass_on(along_z(0), 4).start()
-    if not S2_FIRST:
-        send_opposite()
+    send_opposite()
     for dy, one, two in ((3, 4, 8), (1, 5, 9)):
         if Y_EARLY:
             arrived(one, rows_of(2, dy, 0, 32, columns(0, Y_EARLY)))

time: 56.5 us -> 54.8 us (0.970)
  Pallas kernels: 56.4 us -> 54.7 us
    pallas_call x1, Pallas kernels: 52.3 us -> 50.7 us  [per_device(): pl.pallas_call(factor_kernel, name='factor', out_shape=[jax.ShapeDtypeStr...]
where the time goes in v5:
time: 54.8 us; the launch traced here: 54.7 us
  Pallas kernels  54.7 us (100%)
    pallas_call x1, Pallas kernels, per_device(): pl.pallas_call(factor_kernel, name='factor', out_shape=[jax.ShapeDtypeStr...  50.7 us
    pallas_call x1, Pallas kernels, per_device(): pl.pallas_call(apply_kernel, name='apply', out_shape=jax.ShapeDtypeStruct...  4.03 us

profile of v5, /device:TPU:1, one launch (start us, length us, event | category | flops | bytes accessed | tf_op | source)
XLA Modules:
  0.0 54.7 jit_solution(10620207012170920939)
XLA Ops:
  0.0 50.7 %factor.1 = (bf16[512,8192]{1,0:T(8,128)(2,1)S(1)}, bf16[2,4,4,288,128]{4,3,2,1,0:T(8,128)(2,1)S(1)}) custom-call(bf16[1024,8192]{1,0:T(8,128)(2,1)} %act_ref.1, bf16[32,8192]{1,0:T(8,128)(2,1)} %bitcast.3, s32[32]{0:T(128)} %iters_ref.1), custom_call_target="tpu_custom_call" | custom-call | flops 5000000000 | bytes 33554432 | tf_op jit(solution)/shard_map/factor/pallas_call | solution.py:437
  50.7 4.0 %apply.1 = bf16[8192,512]{1,0:T(8,128)(2,1)} custom-call(bf16[32,288,128]{2,1,0:T(8,128)(2,1)S(1)} %bitcast.2, bf16[512,8192]{1,0:T(8,128)(2,1)S(1)} %get-tuple-element.8.grad_ref), custom_call_target="tpu_custom_call" | custom-call | flops 2000000000 | bytes 20971520 | tf_op jit(solution)/shard_map/apply/pallas_call | solution.py:472

commit v6 on v5

--- a/solution.py
+++ b/solution.py
@@ -21,10 +21,11 @@
 GROUP = 4
 GROUP_COLS = GROUP * BS
 CLASS = 16
-WRITE = 4
+WRITE = 1
 AHEAD = 4
 AWAY = (2, 1, 3, 0)
-X_EARLY = 3072
+X_EARLY = 2048
+MIDDLE = 4096
 Y_EARLY = 2048
 ACROSS = 2048
 MESH = pl.DeviceIdType.MESH
@@ -290,8 +291,8 @@
     for dy in (2, 1, 3):
         y_copy(dy).start()
 
-    if X_EARLY < width:
-        send_parts(3, 2, 0, X_EARLY, width)
+    send_parts(3, 2, 0, X_EARLY, MIDDLE)
+    send_parts(13, 2, 0, MIDDLE, width)
     arrived(0, shard(0, 3))
     gather(6, 0, 1, rows_of(0, 3, 0, 16))
     arrived(1, shard(0, 1))
@@ -300,6 +301,10 @@
     to_sibling(2, shard(0, 1))
     for dy in (1, 3, 2):
         y_copy(dy).wait_recv()
+
+    arrived(3, rows_of(2, 0, 0, 32, columns(X_EARLY, MIDDLE)))
+    send_parts(8, 0, 1, Y_EARLY, MIDDLE, rows_of(2, 0, 0, 32, columns(Y_EARLY, MIDDLE)))
+    send_parts(9, 0, 3, Y_EARLY, MIDDLE, rows_of(2, 0, 0, 32, columns(Y_EARLY, MIDDLE)))
 
     terms = [y_terms[i].astype(jnp.float32) for i in range(SIDE)]
     whole = (terms[0] + terms[1]) + (terms[2] + terms[3])
@@ -344,10 +349,9 @@
     keep = pltpu.make_async_copy(inv_own, inv_ref.at[core, z, x], local_sem.at[1])
     keep.start()
 
-    if X_EARLY < width:
-        arrived(3, rows_of(2, 0, 0, 32, columns(X_EARLY, width)))
-    send_parts(8, 0, 1, Y_EARLY, width, rows_of(2, 0, 0, 32, columns(Y_EARLY, width)))
-    send_parts(9, 0, 3, Y_EARLY, width, rows_of(2, 0, 0, 32, columns(Y_EARLY, width)))
+    arrived(13, rows_of(2, 0, 0, 32, columns(MIDDLE, width)))
+    send_parts(14, 0, 1, MIDDLE, width, rows_of(2, 0, 0, 32, columns(MIDDLE, width)))
+    send_parts(15, 0, 3, MIDDLE, width, rows_of(2, 0, 0, 32, columns(MIDDLE, width)))
     to_sibling(3, shard(2, 0))
     keep.wait()
     for d in (1, 3, 2):
@@ -361,10 +365,11 @@
     pass_on(along_x(0), 0).start()
     pass_on(along_z(0), 4).start()
     send_opposite()
-    for dy, one, two in ((3, 4, 8), (1, 5, 9)):
+    for dy, one, two, three in ((3, 4, 8, 14), (1, 5, 9, 15)):
         if Y_EARLY:
             arrived(one, rows_of(2, dy, 0, 32, columns(0, Y_EARLY)))
-        arrived(two, rows_of(2, dy, 0, 32, columns(Y_EARLY, width)))
+        arrived(two, rows_of(2, dy, 0, 32, columns(Y_EARLY, MIDDLE)))
+        arrived(three, rows_of(2, dy, 0, 32, columns(MIDDLE, width)))
         if ACROSS < width:
             first_row = 0 if dy == 3 else 16
             gather(11 + first_row // 16, 0, 4 - dy, rows_of(2, dy, first_row, 16, columns(ACROSS, width)))
@@ -461,7 +466,7 @@
             dma((8,)), dma((4,)), dma((4,)), dma((3,)), dma((3,)), dma((4, 2)), dma((4, 2)), dma((4,)), dma((4,)),
             dma((4,)), dma((4,)), dma((3,)), dma((3,)),
             dma((4,)), dma((4,)), dma((4,)), dma((4,)), dma((4,)), dma((4,)), dma((4,)), dma((4,)), dma((8,)), dma((8,)),
-            dma((3,)), dma((13,)), dma((13,)), dma((8,)), dma((8,)),
+            dma((3,)), dma((16,)), dma((16,)), dma((8,)), dma((8,)),
         ],
         compiler_params=pltpu.CompilerParams(
             collective_id=0, has_side_effects=True, vmem_limit_bytes=32 << 20

time: 54.8 us -> 53.7 us (0.980)
  Pallas kernels: 54.7 us -> 53.6 us
    pallas_call x1, Pallas kernels: 50.7 us -> 49.8 us  [per_device(): pl.pallas_call(factor_kernel, name='factor', out_shape=[jax.ShapeDtypeStr...]
where the time goes in v6:
time: 53.7 us; the launch traced here: 53.6 us
  Pallas kernels  53.6 us (100%)
    pallas_call x1, Pallas kernels, per_device(): pl.pallas_call(factor_kernel, name='factor', out_shape=[jax.ShapeDtypeStr...  49.8 us
    pallas_call x1, Pallas kernels, per_device(): pl.pallas_call(apply_kernel, name='apply', out_shape=jax.ShapeDtypeStruct...  3.82 us

profile of v6, /device:TPU:1, one launch (start us, length us, event | category | flops | bytes accessed | tf_op | source)
XLA Modules:
  0.0 53.6 jit_solution(10944306358625437140)
XLA Ops:
  0.0 49.8 %factor.1 = (bf16[512,8192]{1,0:T(8,128)(2,1)S(1)}, bf16[2,4,4,288,128]{4,3,2,1,0:T(8,128)(2,1)S(1)}) custom-call(bf16[1024,8192]{1,0:T(8,128)(2,1)} %act_ref.1, bf16[32,8192]{1,0:T(8,128)(2,1)} %bitcast.3, s32[32]{0:T(128)} %iters_ref.1), custom_call_target="tpu_custom_call" | custom-call | flops 5000000000 | bytes 33554432 | tf_op jit(solution)/shard_map/factor/pallas_call | solution.py:442
  49.8 3.8 %apply.1 = bf16[8192,512]{1,0:T(8,128)(2,1)} custom-call(bf16[32,288,128]{2,1,0:T(8,128)(2,1)S(1)} %bitcast.2, bf16[512,8192]{1,0:T(8,128)(2,1)S(1)} %get-tuple-element.8.grad_ref), custom_call_target="tpu_custom_call" | custom-call | flops 2000000000 | bytes 20971520 | tf_op jit(solution)/shard_map/apply/pallas_call | solution.py:477

commit v7 on v6

--- a/solution.py
+++ b/solution.py
@@ -25,7 +25,7 @@
 AHEAD = 4
 AWAY = (2, 1, 3, 0)
 X_EARLY = 2048
-MIDDLE = 4096
+MIDDLE = 5120
 Y_EARLY = 2048
 ACROSS = 2048
 MESH = pl.DeviceIdType.MESH

time: 53.7 us -> 54.3 us (1.011)
  Pallas kernels: 53.6 us -> 54.2 us
    pallas_call x1, Pallas kernels: 49.8 us -> 50.3 us  [per_device(): pl.pallas_call(factor_kernel, name='factor', out_shape=[jax.ShapeDtypeStr...]
where the time goes in v7:
time: 54.3 us; the launch traced here: 54.2 us
  Pallas kernels  54.2 us (100%)
    pallas_call x1, Pallas kernels, per_device(): pl.pallas_call(factor_kernel, name='factor', out_shape=[jax.ShapeDtypeStr...  50.3 us
    pallas_call x1, Pallas kernels, per_device(): pl.pallas_call(apply_kernel, name='apply', out_shape=jax.ShapeDtypeStruct...  3.83 us

profile of v7, /device:TPU:1, one launch (start us, length us, event | category | flops | bytes accessed | tf_op | source)
XLA Modules:
  0.0 54.2 jit_solution(5075460594331779133)
XLA Ops:
  0.0 50.3 %factor.1 = (bf16[512,8192]{1,0:T(8,128)(2,1)S(1)}, bf16[2,4,4,288,128]{4,3,2,1,0:T(8,128)(2,1)S(1)}) custom-call(bf16[1024,8192]{1,0:T(8,128)(2,1)} %act_ref.1, bf16[32,8192]{1,0:T(8,128)(2,1)} %bitcast.3, s32[32]{0:T(128)} %iters_ref.1), custom_call_target="tpu_custom_call" | custom-call | flops 5000000000 | bytes 33554432 | tf_op jit(solution)/shard_map/factor/pallas_call | solution.py:442
  50.3 3.8 %apply.1 = bf16[8192,512]{1,0:T(8,128)(2,1)} custom-call(bf16[32,288,128]{2,1,0:T(8,128)(2,1)S(1)} %bitcast.2, bf16[512,8192]{1,0:T(8,128)(2,1)S(1)} %get-tuple-element.8.grad_ref), custom_call_target="tpu_custom_call" | custom-call | flops 2000000000 | bytes 20971520 | tf_op jit(solution)/shard_map/apply/pallas_call | solution.py:477
